TPU v7x, 32 devices: a whole 2x2x4 slice. The times are simulated.
32 devices in a mesh: rep: 2 (over y), wide: 16 (over z, x, core).
Axes of the slice: x: 2, y: 2, z: 4, core: 2. Of those that a mesh axis runs over, the one named last changes fastest.
Arguments:
- normed_hidden: bfloat16 [4096, 8192], P(('rep', 'wide')), parts along dimension 0, may hold values from -6 to 6
- fresh_queries: bfloat16 [4096, 1024], P(('rep', 'wide')), parts along dimension 0, may hold values from -48 to 48
- fresh_key_value: bfloat16 [4096, 256], P(('rep', 'wide')), parts along dimension 0, may hold values from -6 to 6
- key_value_cache: bfloat16 [4096, 64, 256], P(('rep', 'wide')), parts along dimension 0, may hold values from -16 to 16
- lengths: int32 [4096], P(('rep', 'wide')), parts along dimension 0, may hold values from 2 to 64, as said below
- adapter_choice: int32 [4096], P(('rep', 'wide')), parts along dimension 0, may hold values from 0 to 63, as said below
- low_rank_down: bfloat16 [64, 8192, 128], P('wide'), may hold values from -0.0625 to 0.0625
- low_rank_up: bfloat16 [64, 2, 64, 128], P('wide'), may hold values from -0.75 to 0.75
Outputs:
- new_entry: bfloat16 [4096, 256], P(('rep', 'wide')), parts along dimension 0
- attended: bfloat16 [4096, 1024], P(('rep', 'wide')), parts along dimension 0
There are 2 independent parts, one for each index of `rep`. A program takes and returns all parts, laid end to end along the dimension named above; an argument that names none is the same for every part. Nothing has to cross between parts.
Inputs may be any that keep to these rules, and one draw needn't show every extreme that they name: `adapter_choice`: adapter a is stored on index a // 4 of wide. Among the rows of one device at most 16 name adapters stored on one device, and in every draw the adapters of some device are named by exactly 16 rows of every device. `lengths`: some request uses all 64 positions.
All inputs are finite; a program needn't handle non-finite values.
Results may differ from a plain program's by a relative error of at most 0.0063.
Values may be sent and summed in bfloat16 or wider, within the bound.
A program may use at most 64 MiB of HBM per device.

v0:
```python
import math

import jax
import jax.numpy as jnp
from jax import lax
from jax.sharding import PartitionSpec as P


def apply_low_rank(received_rows, request_labels, low_rank_down, low_rank_up):
    kept_count = low_rank_down.shape[0]
    double_rank = low_rank_down.shape[2]
    senders = received_rows.shape[0]
    per_owner = received_rows.shape[1]
    picked = request_labels[:, :, None] == jnp.arange(kept_count)[None, None, :]
    project_input = jnp.einsum(
        "ikv,hvp->ikhp", received_rows, low_rank_down, preferred_element_type=jnp.float32
    ).astype(jnp.bfloat16)
    project_input = jnp.where(picked[:, :, :, None], project_input, jnp.zeros_like(project_input))
    project_input = project_input.reshape(senders, per_owner, kept_count, 2, double_rank // 2)
    low_rank_update = jnp.einsum(
        "uygwk,gwke->uywe", project_input, low_rank_up, preferred_element_type=jnp.float32
    )
    return low_rank_update.astype(jnp.bfloat16).reshape(senders, per_owner, -1)


def return_rows(low_rank_update):
    return lax.all_to_all(low_rank_update, "wide", split_axis=0, concat_axis=0, tiled=True)


def attend(fresh_queries, key_value_cache, lengths, entry):
    head_size = entry.shape[1] // 2
    requests = fresh_queries.shape[0]
    context = key_value_cache.shape[1]
    queries = fresh_queries.reshape(requests, -1, head_size)
    scores = jnp.einsum(
        "rqh,rch->rqc",
        queries,
        key_value_cache[:, :, :head_size],
        preferred_element_type=jnp.float32,
    ) / math.sqrt(head_size)
    usable = (jnp.arange(context, dtype=jnp.int32)[None, :] < lengths[:, None])[:, None, :]
    scores = jnp.where(usable, scores, -1e30)
    fresh_score = jnp.einsum(
        "rqh,rh->rq", queries, entry[:, :head_size], preferred_element_type=jnp.float32
    ) / math.sqrt(head_size)
    highest = jnp.maximum(jnp.max(scores, axis=2), fresh_score)
    cached_exp = jnp.where(usable, jnp.exp(scores - highest[:, :, None]), 0.0)
    fresh_exp = jnp.exp(fresh_score - highest)
    denominator = jnp.sum(cached_exp, axis=2) + fresh_exp
    cached_weight = (cached_exp / denominator[:, :, None]).astype(jnp.bfloat16)
    fresh_weight = (fresh_exp / denominator).astype(jnp.bfloat16)
    output = jnp.einsum(
        "rqc,rch->rqh",
        cached_weight,
        key_value_cache[:, :, head_size:],
        preferred_element_type=jnp.float32,
    )
    output = output + fresh_weight.astype(jnp.float32)[:, :, None] * entry[
        :, None, head_size:
    ].astype(jnp.float32)
    return output.astype(jnp.bfloat16).reshape(requests, -1)


def shards(
    normed_hidden,
    fresh_queries,
    fresh_key_value,
    key_value_cache,
    lengths,
    adapter_choice,
    low_rank_down,
    low_rank_up,
):
    devices_wide = lax.axis_size("wide")
    requests = normed_hidden.shape[0]
    per_owner = 2 * requests // devices_wide
    kept_count = low_rank_down.shape[0]
    owners = adapter_choice // kept_count
    owner_hit = owners[:, None] == jnp.arange(devices_wide, dtype=jnp.int32)[None, :]
    earlier = jnp.cumsum(owner_hit.astype(jnp.int32), axis=0) - 1
    position = jnp.sum(jnp.where(owner_hit, earlier, 0), axis=1)
    target = owners * per_owner + position
    placing = (
        target[:, None] == jnp.arange(devices_wide * per_owner, dtype=jnp.int32)[None, :]
    ).astype(jnp.bfloat16)
    packed = jnp.einsum(
        "rs,rd->sd", placing, normed_hidden, preferred_element_type=jnp.float32
    ).astype(jnp.bfloat16)
    packed = packed.reshape(devices_wide, per_owner, -1)
    every_id = lax.all_gather(adapter_choice, "wide", axis=0, tiled=True).reshape(
        devices_wide, requests
    )
    mine = every_id // kept_count == lax.axis_index("wide")
    order_mine = jnp.cumsum(mine.astype(jnp.int32), axis=1) - 1
    matched = mine[:, :, None] & (
        order_mine[:, :, None] == jnp.arange(per_owner, dtype=jnp.int32)[None, None, :]
    )
    request_labels = (
        jnp.sum(jnp.where(matched, (every_id % kept_count + 1)[:, :, None], 0), axis=1) - 1
    )
    received_rows = lax.all_to_all(packed, "wide", split_axis=0, concat_axis=0, tiled=True)
    returned_rows = return_rows(
        apply_low_rank(received_rows, request_labels, low_rank_down, low_rank_up)
    )
    flat_back = returned_rows.reshape(devices_wide * per_owner, -1)
    update_rows = jnp.einsum("rs,sh->rh", placing, flat_back, preferred_element_type=jnp.float32)
    new_entry = (fresh_key_value.astype(jnp.float32) + update_rows).astype(jnp.bfloat16)
    attended = attend(fresh_queries, key_value_cache, lengths, new_entry)
    return (new_entry, attended)


def solution(mesh):
    return jax.shard_map(
        shards,
        mesh=mesh,
        in_specs=(
            P(("rep", "wide"), None),
            P(("rep", "wide"), None),
            P(("rep", "wide"), None),
            P(("rep", "wide"), None, None),
            P(("rep", "wide")),
            P(("rep", "wide")),
            P("wide", None, None),
            P("wide", None, None, None),
        ),
        out_specs=(P(("rep", "wide"), None), P(("rep", "wide"), None)),
        check_vma=False,
    )
```

profile of v0, /device:TPU:0, one launch (start us, length us, event | category | flops | bytes accessed | tf_op | source)
XLA Modules:
  0.0 141.7 jit_solution(2363917255338968807)
XLA Ops:
  0.6 0.8 and_select_fusion
  1.5 0.2 reduce_window_sum.22
  1.7 0.2 select_reduce_fusion.1
  1.9 0.7 multiply_add_fusion
  2.6 3.3 %convolution_convert_fusion = bf16[256,8192]{1,0:T(8,128)(2,1)} fusion(bf16[128,8192]{1,0:T(8,128)(2,1)S(1)} %copy-done, s32[128]{0:T(128)S(1)} %multiply_add_fusion), kind=kOutput, calls=%fused_computation | convolution fusion | flops 539000832 | bytes 6291968 | tf_op jit(solution)/shard_map/rs,rd->sd/dot_general | solution.py:86
  5.9 7.5 %all-to-all-start = ((bf16[16,16,8192]{2,1,0:T(8,128)(2,1)}), bf16[16,16,8192]{2,1,0:T(8,128)(2,1)}, u32[]{:S(2)}, u32[]{:S(2)}) async-start(bf16[16,16,8192]{2,1,0:T(8,128)(2,1)} %bitcast.69), calls=%async_computation | async-start | bytes 8388608 | tf_op jit(solution)/shard_map/all_to_all | solution.py:101
  13.5 83.9 %all-gather = s32[16,1,128]{2,1,0:T(1,128)S(1)} all-gather(s32[1,1,128]{2,1,0:T(1,128)S(1)} %bitcast.78), channel_id=1, replica_groups=mesh['rep'=2,'wide'=16] {'wide'}, dimensions={0}, use_global_device_ids=true | all-gather | bytes 8704 | tf_op jit(solution)/shard_map/all_gather | solution.py:90
  97.3 0.3 reduce_window_sum.23
  97.7 0.3 select_reduce_fusion
  98.2 7.0 %fusion.25 = bf16[16,16,4,128]{3,1,2,0:T(8,128)(2,1)S(1)} fusion(bf16[4,8192,128]{2,1,0:T(8,128)(2,1)} %param.14, bf16[16,16,8192]{2,1,0:T(8,128)(2,1)} %all-to-all-done, pred[16,16,4]{1,2,0:T(4,128)(4,1)S(1)} %iota_compare_fusion.6), kind=kOutput, calls=%fused_computation.15 | convolution fusion | flops 2147745792 | bytes 12846080 | tf_op jit(solution)/shard_map/ikv,hvp->ikhp/dot_general | solution.py:15
  105.2 0.2 reshape.144
  105.5 0.3 fusion.30
  105.8 0.7 copy.56
  106.5 22.8 %all-to-all-start.1 = ((bf16[16,16,256]{2,1,0:T(8,128)(2,1)}), bf16[16,16,256]{2,1,0:T(8,128)(2,1)S(1)}, u32[]{:S(2)}, u32[]{:S(2)}) async-start(bf16[16,16,256]{2,1,0:T(8,128)(2,1)} %bitcast.68), calls=%async_computation.1 | async-start | bytes 262144 | tf_op jit(solution)/shard_map/all_to_all | solution.py:27
  129.2 2.9 %fusion.55 = (f32[128,8]{1,0:T(8,128)S(1)}, f32[128,8,64]{2,1,0:T(8,128)S(1)}) fusion(bf16[128,8,128]{2,1,0:T(8,128)(2,1)S(1)} %bitcast.70, bf16[128,64,256]{2,1,0:T(8,128)(2,1)} %param.11, pred[128,64]{1,0:T(8,128)(4,1)S(1)} %iota_compare_fusion.4), kind=kOutput, calls=%fused_computation.70 | convolution fusion | flops 16972800 | bytes 2633728 | tf_op jit(solution)/shard_map/rqh,rch->rqc/dot_general | solution.py:35
  132.1 5.0 %all-to-all-done.1 = bf16[16,16,256]{2,1,0:T(8,128)(2,1)S(1)} async-done(((bf16[16,16,256]{2,1,0:T(8,128)(2,1)}), bf16[16,16,256]{2,1,0:T(8,128)(2,1)S(1)}, u32[]{:S(2)}, u32[]{:S(2)}) %all-to-all-start.1) | async-done | bytes 131104 | tf_op jit(solution)/shard_map/all_to_all | solution.py:27
  137.2 0.2 fusion.31
  137.4 0.3 fusion.43
  137.7 0.1 copy.33
  137.9 0.4 fusion.33
  138.3 0.1 copy.36
  138.4 0.1 copy.35
  138.5 2.4 %fusion.16 = bf16[128,8,128]{2,1,0:T(8,128)(2,1)S(1)} fusion(bf16[128,64,256]{2,1,0:T(8,128)(2,1)} %param.11, f32[128,8,64]{2,1,0:T(8,128)S(1)} %get-tuple-element.9, f32[128,128]{1,0:T(8,128)S(1)} %get-tuple-element.5, f32[128,8]{1,0:T(8,128)S(1)} %copy.36, f32[128,8]{1,0:T(8,128)S(1)} %copy.35, f32[128,8]{1,0:T(8,128)S(1)} %copy.33, ...), kind=kOutput, calls=%fused_computation.11 | convolution fusion | flops 17432576 | bytes 2707456 | tf_op jit(solution)/shard_map/rqc,rch->rqh/dot_general | solution.py:52
  140.9 0.8 copy.55
  (28 shorter events, 0.5 us)
Async XLA Ops:
  0.6 1.9 %copy-start = (bf16[128,8192]{1,0:T(8,128)(2,1)S(1)}, bf16[128,8192]{1,0:T(8,128)(2,1)}, u32[]{:S(2)}) copy-start(bf16[128,8192]{1,0:T(8,128)(2,1)} %param.8) | copy-start | bytes 6291460
  5.9 7.6 %copy-start.4 = (s32[128]{0:T(128)S(1)}, s32[128]{0:T(128)}, u32[]{:S(2)}) copy-start(s32[128]{0:T(128)} %param.13) | copy-start | bytes 1540
  5.9 91.7 %copy-start.1 = (bf16[128,1024]{1,0:T(8,128)(2,1)S(1)}, bf16[128,1024]{1,0:T(8,128)(2,1)}, u32[]{:S(2)}) copy-start(bf16[128,1024]{1,0:T(8,128)(2,1)} %param.9) | copy-start | bytes 786436
  5.9 92.2 %copy-start.5 = (s32[128]{0:T(128)S(1)}, s32[128]{0:T(128)}, u32[]{:S(2)}) copy-start(s32[128]{0:T(128)} %param.12) | copy-start | bytes 1540
  5.9 92.3 %all-to-all-start = ((bf16[16,16,8192]{2,1,0:T(8,128)(2,1)}), bf16[16,16,8192]{2,1,0:T(8,128)(2,1)}, u32[]{:S(2)}, u32[]{:S(2)}) async-start(bf16[16,16,8192]{2,1,0:T(8,128)(2,1)} %bitcast.69), calls=%async_computation | async-start | bytes 8388608 | tf_op jit(solution)/shard_map/all_to_all | solution.py:101
  98.2 7.3 %copy-start.6 = (bf16[4,2,64,128]{3,2,1,0:T(8,128)(2,1)S(1)}, bf16[4,2,64,128]{3,2,1,0:T(8,128)(2,1)}, u32[]{:S(2)}) copy-start(bf16[4,2,64,128]{3,2,1,0:T(8,128)(2,1)} %param.15) | copy-start | bytes 393220
  105.2 31.9 %copy-start.3 = (bf16[128,256]{1,0:T(8,128)(2,1)S(1)}, bf16[128,256]{1,0:T(8,128)(2,1)}, u32[]{:S(2)}) copy-start(bf16[128,256]{1,0:T(8,128)(2,1)} %param.10) | copy-start | bytes 196612
  106.5 30.7 %all-to-all-start.1 = ((bf16[16,16,256]{2,1,0:T(8,128)(2,1)}), bf16[16,16,256]{2,1,0:T(8,128)(2,1)S(1)}, u32[]{:S(2)}, u32[]{:S(2)}) async-start(bf16[16,16,256]{2,1,0:T(8,128)(2,1)} %bitcast.68), calls=%async_computation.1 | async-start | bytes 262144 | tf_op jit(solution)/shard_map/all_to_all | solution.py:27
  137.4 4.3 %copy-start.2 = (bf16[128,256]{1,0:T(8,128)(2,1)}, bf16[128,256]{1,0:T(8,128)(2,1)S(1)}, u32[]{:S(2)}) copy-start(bf16[128,256]{1,0:T(8,128)(2,1)S(1)} %fusion.31) | copy-start | bytes 196612
where the time goes:
time: 142 us
  blocking collectives  83.9 us (59%)
  starting transfers between devices  30.3 us (21%)
  matrix products  16.3 us (11%)
  waiting for transfers between devices  5.02 us (4%)
  other arithmetic  3.08 us (2%)
  local copies, waits for them, and re-layouts  2.25 us (2%)
    all_gather x1, blocking collectives, shards(): lax.all_gather(adapter_choice, 'wide', axis=0, tiled=True)  83.9 us
    all_to_all x1, starting transfers between devices, return_rows(): lax.all_to_all(low_rank_update, 'wide', split_axis=0, concat_axis=0, tile...  22.8 us
    all_to_all x1, starting transfers between devices, shards(): lax.all_to_all(packed, 'wide', split_axis=0, concat_axis=0, tiled=True)  7.54 us
    dot_general x1, matrix products, apply_low_rank(): jnp.einsum('ikv,hvp->ikhp', received_rows, low_rank_down, preferred_eleme...  7.01 us
    all_to_all x1, waiting for transfers between devices, return_rows(): lax.all_to_all(low_rank_update, 'wide', split_axis=0, concat_axis=0, tile...  5.02 us
    dot_general x1, matrix products, shards(): jnp.einsum('rs,rd->sd', placing, normed_hidden, preferred_element_type=jn...  3.33 us
    dot_general x1, matrix products, attend(): jnp.einsum('rqh,rch->rqc', queries, key_value_cache[:, :, :head_size], pr...  2.87 us
  transfers between devices with their start and end apart: 2, of which 1 were waited for; matrix products, arithmetic and copies ran while one was open for 3% of the time, Pallas kernels for 0%

commit v1 on v0

--- a/solution.py
+++ b/solution.py
@@ -1,9 +1,14 @@
+import functools
 import math
 
 import jax
 import jax.numpy as jnp
 from jax import lax
+from jax.experimental import pallas as pl
+from jax.experimental.pallas import tpu as pltpu
 from jax.sharding import PartitionSpec as P
+
+CHUNKS = 4
 
 
 def apply_low_rank(received_rows, request_labels, low_rank_down, low_rank_up):
@@ -108,10 +113,340 @@
     attended = attend(fresh_queries, key_value_cache, lengths, new_entry)
     return (new_entry, attended)
 
+def wide_kernel(
+    n,
+    ids_ref,
+    lengths_ref,
+    hidden_ref,
+    queries_ref,
+    fresh_ref,
+    cache_ref,
+    down_ref,
+    up_ref,
+    entry_ref,
+    attended_ref,
+    hidden,
+    cache,
+    down,
+    up,
+    packed,
+    received,
+    labels_out,
+    labels_in,
+    update_out,
+    update_in,
+    placing,
+    placing_t,
+    queries,
+    context_sum,
+    highest,
+    total,
+    project,
+    load_sem,
+    self_sem,
+    send_sem,
+    recv_sem,
+):
+    chunks, per_owner, width = packed.shape[0], packed.shape[2], packed.shape[3]
+    kept = up_ref.shape[0]
+    rank = up_ref.shape[2]
+    head = up_ref.shape[3]
+    requests = ids_ref.shape[1]
+    heads = queries.shape[1]
+    slots = n * per_owner
+    stride = 7 if n % 2 == 0 and n % 7 else 1
+    me = lax.axis_index("wide")
+    f32, bf16 = jnp.float32, jnp.bfloat16
+
+    def columns(c):
+        return pl.ds(pl.multiple_of(c * width, width), width)
+
+    def hidden_load(c):
+        return pltpu.make_async_copy(
+            hidden_ref.at[:, columns(c)], hidden.at[c], load_sem.at[c]
+        )
+
+    def down_load(g):
+        return pltpu.make_async_copy(
+            down_ref.at[g], down.at[:, pl.ds(g * 2 * rank, 2 * rank)], load_sem.at[chunks + g]
+        )
+
+    cache_load = pltpu.make_async_copy(cache_ref, cache, load_sem.at[chunks + kept])
+
+    for c in range(chunks):
+        hidden_load(c).start()
+    cache_load.start()
+    for g in range(kept):
+        down_load(g).start()
+
+    barrier = pltpu.get_barrier_semaphore()
+
+    @pl.loop(1, n)
+    def _(k):
+        pl.semaphore_signal(
+            barrier,
+            inc=1,
+            device_id={"wide": lax.rem(me + k, n)},
+            device_id_type=pl.DeviceIdType.MESH,
+        )
+
+    ids = ids_ref[...]
+    adapter = lax.broadcasted_iota(jnp.int32, (n * kept, requests), 0)
+    named = jnp.where(adapter == ids, 1.0, 0.0).astype(bf16)
+    group_of = lax.broadcasted_iota(jnp.int32, (n, n * kept), 1)
+    first = lax.broadcasted_iota(jnp.int32, (n, n * kept), 0) * kept
+    grouping = jnp.where((group_of >= first) & (group_of < first + kept), 1.0, 0.0).astype(bf16)
+    hit = jnp.dot(grouping, named, preferred_element_type=f32)
+    before = lax.broadcasted_iota(jnp.int32, (requests, requests), 0)
+    after = lax.broadcasted_iota(jnp.int32, (requests, requests), 1)
+    earlier = jnp.dot(
+        hit.astype(bf16),
+        jnp.where(before < after, 1.0, 0.0).astype(bf16),
+        preferred_element_type=f32,
+    )
+    position = jnp.where(hit > 0.5, earlier, -1.0).astype(jnp.int32)
+    place = lax.broadcasted_iota(jnp.int32, (n, per_owner, requests), 1)
+    chosen = jnp.where(place == position[:, None, :], 1.0, 0.0).reshape(slots, requests)
+    placing[...] = chosen.astype(bf16)
+    owner_row = jnp.sum(
+        hit * lax.broadcasted_iota(jnp.int32, (n, requests), 0).astype(f32), axis=0, keepdims=True
+    )
+    within = ids - kept * owner_row.astype(jnp.int32)
+    lane = lax.broadcasted_iota(jnp.int32, (128, requests), 0)
+    flags = jnp.where(lane == within, 1.0, 0.0).astype(bf16)
+    labels = lax.dot_general(
+        placing[...], flags, (((1,), (1,)), ((), ())), preferred_element_type=f32
+    )
+    labels_out[...] = labels.astype(bf16).reshape(n, per_owner, 128)
+    labels_in[me] = labels_out[me]
+
+    pl.semaphore_wait(barrier, n - 1)
+
+    def send(source, target, row, k):
+        return pltpu.make_async_remote_copy(
+            src_ref=source,
+            dst_ref=target,
+            send_sem=send_sem.at[row, k],
+            recv_sem=recv_sem.at[row, k],
+            device_id={"wide": lax.rem(me + k, n)},
+            device_id_type=pl.DeviceIdType.MESH,
+        )
+
+    def row_copy(c, k):
+        return send(packed.at[c, lax.rem(me + k, n)], received.at[c, me], c, k)
+
+    def label_copy(k):
+        return send(labels_out.at[lax.rem(me + k, n)], labels_in.at[me], chunks, k)
+
+    def update_copy(k):
+        return send(update_out.at[lax.rem(me + k, n)], update_in.at[me], chunks + 1, k)
+
+    def self_copy(c):
+        return pltpu.make_async_copy(packed.at[c, me], received.at[c, me], self_sem.at[c])
+
+    step = min(width, 512)
+    for c in range(chunks):
+        hidden_load(c).wait()
+
+        @pl.loop(0, width // step)
+        def _(j):
+            part = pl.ds(pl.multiple_of(j * step, step), step)
+            rows = jnp.dot(placing[...], hidden[c, :, part], preferred_element_type=f32)
+            packed[c, :, :, part] = rows.astype(bf16).reshape(n, per_owner, step)
+
+        self_copy(c).start()
+
+        @pl.loop(1, n)
+        def _(j):
+            row_copy(c, lax.rem(j * stride, n)).start()
+
+        if c == 0:
+
+            @pl.loop(1, n)
+            def _(k):
+                label_copy(k).start()
+
+    placing_t[...] = chosen.T.astype(bf16)
+    up[...] = jnp.zeros_like(up)
+    for g in range(kept):
+        for t in range(2):
+            up[pl.ds((2 * g + t) * rank, rank), pl.ds(t * head, head)] = up_ref[g, t]
+    for h in range(heads):
+        queries[:, h, :] = queries_ref[:, pl.ds(h * head, head)].astype(f32)
+    cache_load.wait()
+    context = cache.shape[1]
+    group = 8 if requests % 8 == 0 else 1
+
+    @pl.loop(0, requests // group)
+    def _(i):
+        for u in range(group):
+            r = i * group + u
+            scores = lax.dot_general(
+                queries[r].astype(bf16),
+                cache[r, :, pl.ds(0, head)],
+                (((1,), (1,)), ((), ())),
+                preferred_element_type=f32,
+            ) / math.sqrt(head)
+            usable = lax.broadcasted_iota(jnp.int32, (heads, context), 1) < lengths_ref[r]
+            scores = jnp.where(usable, scores, -1e30)
+            top = jnp.max(scores, axis=1, keepdims=True)
+            powers = jnp.where(usable, jnp.exp(scores - top), 0.0)
+            highest[r] = jnp.broadcast_to(top, (heads, head))
+            total[r] = jnp.broadcast_to(jnp.sum(powers, axis=1, keepdims=True), (heads, head))
+            context_sum[r] = jnp.dot(
+                powers.astype(bf16), cache[r, :, pl.ds(head, head)], preferred_element_type=f32
+            )
+
+    for g in range(kept):
+        down_load(g).wait()
+
+    for c in range(chunks):
+        self_copy(c).wait()
+
+        @pl.loop(1, n)
+        def _(j):
+            row_copy(c, lax.rem(j * stride, n)).wait_recv()
+
+        product = jnp.dot(
+            received[c].reshape(slots, width),
+            down[pl.ds(c * width, width), :],
+            preferred_element_type=f32,
+        )
+        if c == 0:
+            project[...] = product
+        else:
+            project[...] += product
+
+    @pl.loop(1, n)
+    def _(k):
+        label_copy(k).wait_recv()
+
+    picked = labels_in[...].reshape(slots, 128).astype(f32)
+    masked = [
+        project[:, pl.ds(g * 2 * rank, 2 * rank)] * picked[:, g : g + 1] for g in range(kept)
+    ]
+    update = jnp.dot(
+        jnp.concatenate(masked, axis=1).astype(bf16), up[...], preferred_element_type=f32
+    )
+    update_out[...] = update.astype(bf16).reshape(n, per_owner, 2 * head)
+
+    @pl.loop(1, n)
+    def _(k):
+        update_copy(k).start()
+
+    update_in[me] = update_out[me]
+
+    @pl.loop(1, n)
+    def _(k):
+        update_copy(k).wait_recv()
+
+    back = jnp.dot(
+        placing_t[...], update_in[...].reshape(slots, 2 * head), preferred_element_type=f32
+    )
+    entry = (fresh_ref[...].astype(f32) + back).astype(bf16)
+    entry_ref[...] = entry
+    key = entry[:, :head].astype(f32)
+    value = entry[:, head:].astype(f32)
+    fresh_score = jnp.sum(queries[...] * key[:, None, :], axis=2, keepdims=True) / math.sqrt(head)
+    old = highest[...]
+    new = jnp.maximum(old, fresh_score)
+    scale = jnp.exp(old - new)
+    fresh_power = jnp.exp(fresh_score - new)
+    context_sum[...] = (context_sum[...] * scale + fresh_power * value[:, None, :]) / (
+        total[...] * scale + fresh_power
+    )
+    for h in range(heads):
+        attended_ref[:, pl.ds(h * head, head)] = context_sum[:, h, :].astype(bf16)
+
+    @pl.loop(1, n)
+    def _(k):
+        for c in range(chunks):
+            row_copy(c, k).wait_send()
+        label_copy(k).wait_send()
+        update_copy(k).wait_send()
+
+
+def fused(
+    normed_hidden,
+    fresh_queries,
+    fresh_key_value,
+    key_value_cache,
+    lengths,
+    adapter_choice,
+    low_rank_down,
+    low_rank_up,
+):
+    n = lax.axis_size("wide")
+    requests, model = normed_hidden.shape
+    per_owner = 2 * requests // n
+    kept, _, double_rank = low_rank_down.shape
+    head = low_rank_up.shape[3]
+    heads = fresh_queries.shape[1] // head
+    context = key_value_cache.shape[1]
+    slots = n * per_owner
+    chunks = CHUNKS
+    width = model // chunks
+    bf16, f32 = jnp.bfloat16, jnp.float32
+    vmem = pl.BlockSpec(memory_space=pltpu.VMEM)
+    smem = pl.BlockSpec(memory_space=pltpu.SMEM)
+    anywhere = pl.BlockSpec(memory_space=pl.ANY)
+    return pl.pallas_call(
+        functools.partial(wide_kernel, n),
+        out_shape=(
+            jax.ShapeDtypeStruct((requests, 2 * head), bf16),
+            jax.ShapeDtypeStruct((requests, heads * head), bf16),
+        ),
+        in_specs=[vmem, smem, anywhere, vmem, vmem, anywhere, anywhere, vmem],
+        out_specs=(vmem, vmem),
+        scratch_shapes=[
+            pltpu.VMEM((chunks, requests, width), bf16),
+            pltpu.VMEM((requests, context, 2 * head), bf16),
+            pltpu.VMEM((model, kept * double_rank), bf16),
+            pltpu.VMEM((kept * double_rank, 2 * head), bf16),
+            pltpu.VMEM((chunks, n, per_owner, width), bf16),
+            pltpu.VMEM((chunks, n, per_owner, width), bf16),
+            pltpu.VMEM((n, per_owner, 128), bf16),
+            pltpu.VMEM((n, per_owner, 128), bf16),
+            pltpu.VMEM((n, per_owner, 2 * head), bf16),
+            pltpu.VMEM((n, per_owner, 2 * head), bf16),
+            pltpu.VMEM((slots, requests), bf16),
+            pltpu.VMEM((requests, slots), bf16),
+            pltpu.VMEM((requests, heads, head), f32),
+            pltpu.VMEM((requests, heads, head), f32),
+            pltpu.VMEM((requests, heads, head), f32),
+            pltpu.VMEM((requests, heads, head), f32),
+            pltpu.VMEM((slots, kept * double_rank), f32),
+            pltpu.SemaphoreType.DMA((chunks + kept + 1,)),
+            pltpu.SemaphoreType.DMA((chunks,)),
+            pltpu.SemaphoreType.DMA((chunks + 2, n)),
+            pltpu.SemaphoreType.DMA((chunks + 2, n)),
+        ],
+        compiler_params=pltpu.CompilerParams(
+            collective_id=0, has_side_effects=True, vmem_limit_bytes=56 * 1024 * 1024
+        ),
+    )(
+        adapter_choice.reshape(1, requests),
+        lengths,
+        normed_hidden,
+        fresh_queries,
+        fresh_key_value,
+        key_value_cache,
+        low_rank_down,
+        low_rank_up,
+    )
+
+
+def device_step(*blocks):
+    requests = blocks[0].shape[0]
+    per_owner = 2 * requests // lax.axis_size("wide")
+    if per_owner % 16:
+        return shards(*blocks)
+    return fused(*blocks)
+
 
 def solution(mesh):
     return jax.shard_map(
-        shards,
+        device_step,
         mesh=mesh,
         in_specs=(
             P(("rep", "wide"), None),

time: 142 us -> 114 us (0.80)
  Pallas kernels: 0 us -> 110 us
  blocking collectives: 83.9 us -> 0 us
  starting transfers between devices: 30.3 us -> 0 us
  matrix products: 16.3 us -> 0 us
  waiting for transfers between devices: 5.02 us -> 0 us
  other arithmetic: 3.08 us -> 0 us
    pallas_call x0 -> x1, Pallas kernels: none -> 110 us  [fused(): pl.pallas_call(functools.partial(wide_kernel, n), out_shape=(jax.ShapeDty...]
    all_gather x1 -> x0, blocking collectives: 83.9 us -> none  [shards(): lax.all_gather(adapter_choice, 'wide', axis=0, tiled=True)]
    all_to_all x2 -> x0, starting transfers between devices: 30.3 us -> none  [the longest x1 22.8 us: return_rows(): lax.all_to_all(low_rank_update, 'wide', split_axis=0, concat_axis=0, tile...]
    dot_general x7 -> x0, matrix products: 16.3 us -> none  [the longest x1 7.01 us: apply_low_rank(): jnp.einsum('ikv,hvp->ikhp', received_rows, low_rank_down, preferred_eleme...]
    all_to_all x2 -> x0, waiting for transfers between devices: 5.02 us -> none  [the longest x1 5.02 us: return_rows(): lax.all_to_all(low_rank_update, 'wide', split_axis=0, concat_axis=0, tile...]
    unnamed x16 -> x2, local copies, waits for them, and re-layouts: 0.84 us -> 3.14 us
  transfers between devices with their start and end apart: 2 -> 0, of which waited for: 1 -> 0; matrix products, arithmetic and copies ran while one was open for 3% -> 0% of each run, Pallas kernels for 0% -> 0%
where the time goes in v1:
time: 114 us
  Pallas kernels  110 us (96%)
  local copies, waits for them, and re-layouts  3.14 us (3%)
    pallas_call x1, Pallas kernels, fused(): pl.pallas_call(functools.partial(wide_kernel, n), out_shape=(jax.ShapeDty...  110 us
    unnamed x2, local copies, waits for them, and re-layouts  3.14 us

profile of v1, /device:TPU:0, one launch (start us, length us, event | category | flops | bytes accessed | tf_op | source)
XLA Modules:
  0.0 114.3 jit_solution(13079104450937518256)
XLA Ops:
  0.6 110.5 %shard_map.95 = (bf16[128,256]{1,0:T(8,128)(2,1)}, bf16[128,1024]{1,0:T(8,128)(2,1)}) custom-call(s32[1,128]{1,0:T(1,128)} %bitcast.1, s32[128]{0:T(128)} %lengths_ref.1, bf16[128,8192]{1,0:T(8,128)(2,1)} %hidden_ref.1, bf16[128,1024]{1,0:T(8,128)(2,1)} %queries_ref.1, bf16[128,256]{1,0:T(8,128)(2,1)} %fresh_ref.1, bf16[128,64,256]{2,1,0:T(8,128)(2,1)} %cache_ref.1, ...), custom_call_target="tpu_custom_call" | custom-call | tf_op jit(solution)/shard_map/pallas_call | solution.py:393
  111.1 1.5 %copy.12 = bf16[128,256]{1,0:T(8,128)(2,1)} copy(bf16[128,256]{1,0:T(8,128)(2,1)} %get-tuple-element.4) | data formatting | bytes 131072
  112.6 1.7 %copy.13 = bf16[128,1024]{1,0:T(8,128)(2,1)} copy(bf16[128,1024]{1,0:T(8,128)(2,1)} %get-tuple-element.5) | data formatting | bytes 524288

commit v2 on v1

--- a/solution.py
+++ b/solution.py
@@ -9,6 +9,7 @@
 from jax.sharding import PartitionSpec as P
 
 CHUNKS = 4
+HALF_CHUNKS = 8
 
 
 def apply_low_rank(received_rows, request_labels, low_rank_down, low_rank_up):
@@ -436,12 +437,647 @@
     )
 
 
+def half_kernel(
+    n,
+    reps,
+    ids_ref,
+    lengths_ref,
+    hidden_ref,
+    queries_ref,
+    fresh_ref,
+    cache_ref,
+    down_ref,
+    up_ref,
+    entry_ref,
+    attended_ref,
+    over_ref,
+    hidden,
+    cache,
+    down,
+    up,
+    cross_out,
+    cross_in,
+    direct_out,
+    forward,
+    received,
+    label_cross_out,
+    label_cross_in,
+    label_direct_out,
+    label_forward,
+    label_received,
+    update,
+    update_direct,
+    update_relay,
+    back_out,
+    back_in,
+    over_out,
+    over_in,
+    over_rep_out,
+    over_rep_in,
+    direct_place,
+    direct_t,
+    cross_place,
+    cross_t,
+    relay_place,
+    relay_t,
+    queries,
+    context_sum,
+    highest,
+    total,
+    project,
+    load_sem,
+    self_sem,
+    cross_send,
+    cross_recv,
+    direct_send,
+    direct_recv,
+    forward_send,
+    forward_recv,
+    update_send,
+    update_recv,
+    relay_send,
+    relay_recv,
+    back_send,
+    back_recv,
+    over_send,
+    over_recv,
+    rep_send,
+    rep_recv,
+):
+    chunks, limit, width = cross_out.shape
+    inner = n // 2
+    lanes = n // 4
+    per_owner = direct_out.shape[2]
+    kept, _, rank, head = up_ref.shape
+    requests = ids_ref.shape[1]
+    heads = queries.shape[1]
+    slots = n * per_owner
+    half_slots = inner * per_owner
+    half_adapters = inner * kept
+    f32, bf16 = jnp.float32, jnp.bfloat16
+    nt = (((1,), (1,)), ((), ()))
+
+    me = lax.axis_index("wide")
+    rep = lax.axis_index("rep")
+    plane = me // lanes
+    lane = lax.rem(me, lanes)
+    half = me // inner
+    mine = lax.rem(me, inner)
+    far = (1 - half) * 2
+    is_relay = plane == 1 + half
+    relay_row = (1 + half) * lanes
+
+    def columns(c):
+        return pl.ds(pl.multiple_of(c * width, width), width)
+
+    def hidden_load(c):
+        return pltpu.make_async_copy(
+            hidden_ref.at[:, columns(c)], hidden.at[c], load_sem.at[c]
+        )
+
+    def down_load(g):
+        return pltpu.make_async_copy(
+            down_ref.at[g], down.at[:, pl.ds(g * 2 * rank, 2 * rank)], load_sem.at[chunks + g]
+        )
+
+    cache_load = pltpu.make_async_copy(cache_ref, cache, load_sem.at[chunks + kept])
+
+    barrier = pltpu.get_barrier_semaphore()
+
+    @pl.loop(1, n)
+    def _(k):
+        pl.semaphore_signal(
+            barrier,
+            inc=1,
+            device_id={"wide": lax.rem(me + k, n)},
+            device_id_type=pl.DeviceIdType.MESH,
+        )
+
+    for k in range(1, reps):
+        pl.semaphore_signal(
+            barrier,
+            inc=1,
+            device_id={"rep": lax.rem(rep + k, reps)},
+            device_id_type=pl.DeviceIdType.MESH,
+        )
+
+    for c in range(chunks):
+        hidden_load(c).start()
+    cache_load.start()
+    for g in range(kept):
+        down_load(g).start()
+
+    def remote(source, target, send_sem, recv_sem, wide):
+        return pltpu.make_async_remote_copy(
+            src_ref=source,
+            dst_ref=target,
+            send_sem=send_sem,
+            recv_sem=recv_sem,
+            device_id={"wide": wide},
+            device_id_type=pl.DeviceIdType.MESH,
+        )
+
+    def peer(k):
+        return half * inner + lax.rem(mine + k, inner)
+
+    def cross_copy(c, b):
+        source = label_cross_out if c is None else cross_out.at[c]
+        target = label_cross_in.at[b] if c is None else cross_in.at[c, b]
+        t = chunks if c is None else c
+        return remote(
+            source, target, cross_send.at[t], cross_recv.at[t, b], (2 - half) * lanes + lane
+        )
+
+    def direct_copy(c, k):
+        to = peer(k)
+        there = lax.rem(to, inner)
+        source = label_direct_out.at[there] if c is None else direct_out.at[c, there]
+        target = label_received.at[plane, lane] if c is None else received.at[c, plane, lane]
+        t = chunks if c is None else c
+        return remote(source, target, direct_send.at[t, k], direct_recv.at[t, k], to)
+
+    def forward_copy(c, k, from_lane):
+        to = peer(k)
+        there = lax.rem(to, inner)
+        source = label_forward.at[there] if c is None else forward.at[c, there]
+        rows = pl.ds(far, 2)
+        if c is None:
+            target = label_received.at[rows, from_lane]
+        else:
+            target = received.at[c, rows, from_lane]
+        t = chunks if c is None else c
+        return remote(source, target, forward_send.at[t, k], forward_recv.at[t, from_lane], to)
+
+    def self_copy(c):
+        return pltpu.make_async_copy(
+            direct_out.at[c, mine], received.at[c, plane, lane], self_sem.at[0, c]
+        )
+
+    def self_forward(c):
+        return pltpu.make_async_copy(
+            forward.at[c, mine], received.at[c, pl.ds(far, 2), lane], self_sem.at[1, c]
+        )
+
+    def update_copy(k):
+        to = peer(k)
+        return remote(
+            update.at[to // lanes, lax.rem(to, lanes)],
+            update_direct.at[mine],
+            update_send.at[k],
+            update_recv.at[k],
+            to,
+        )
+
+    def relay_copy(to_lane, owner):
+        return remote(
+            update.at[pl.ds(far, 2), to_lane],
+            update_relay.at[owner],
+            relay_send.at[to_lane],
+            relay_recv.at[owner],
+            relay_row + to_lane,
+        )
+
+    def back_copy(b):
+        return remote(
+            back_out.at[b], back_in, back_send.at[b], back_recv.at[0], (far + b) * lanes + lane
+        )
+
+    def over_copy(k):
+        return remote(
+            over_out, over_in.at[me], over_send.at[k], over_recv.at[k], lax.rem(me + k, n)
+        )
+
+    def rep_copy(k):
+        return pltpu.make_async_remote_copy(
+            src_ref=over_rep_out,
+            dst_ref=over_rep_in.at[rep],
+            send_sem=rep_send.at[k],
+            recv_sem=rep_recv.at[k],
+            device_id={"rep": lax.rem(rep + k, reps)},
+            device_id_type=pl.DeviceIdType.MESH,
+        )
+
+    def ranks(hit):
+        size = hit.shape[1]
+        before = lax.broadcasted_iota(jnp.int32, (size, size), 0)
+        after = lax.broadcasted_iota(jnp.int32, (size, size), 1)
+        earlier = jnp.dot(
+            hit.astype(bf16),
+            jnp.where(before < after, 1.0, 0.0).astype(bf16),
+            preferred_element_type=f32,
+        )
+        return jnp.where(hit > 0.5, earlier, -1.0).astype(jnp.int32)
+
+    def spread(hit):
+        size = hit.shape[1]
+        place = lax.broadcasted_iota(jnp.int32, (inner, per_owner, size), 1)
+        chosen = jnp.where(place == ranks(hit)[:, None, :], 1.0, 0.0)
+        return chosen.reshape(half_slots, size)
+
+    ids = ids_ref[...]
+    near = ids - half * half_adapters
+    group_of = lax.broadcasted_iota(jnp.int32, (inner, 128), 1)
+    first = lax.broadcasted_iota(jnp.int32, (inner, 128), 0) * kept
+    grouping = jnp.where((group_of >= first) & (group_of < first + kept), 1.0, 0.0).astype(bf16)
+    label_lane = lax.broadcasted_iota(jnp.int32, (128, requests), 0)
+    near_flags = jnp.where(label_lane == near, 1.0, 0.0).astype(bf16)
+    far_flags = jnp.where(
+        label_lane == ids - (1 - half) * half_adapters, 1.0, 0.0
+    ).astype(bf16)
+    hit = jnp.dot(grouping, near_flags, preferred_element_type=f32)
+    direct = spread(hit)
+    direct_place[...] = direct.astype(bf16)
+    crossing = 1.0 - jnp.sum(hit, axis=0, keepdims=True)
+    cross_rank = ranks(jnp.broadcast_to(crossing, (8, requests)))[0:1, :]
+    cross = jnp.where(
+        lax.broadcasted_iota(jnp.int32, (limit, requests), 0) == cross_rank, 1.0, 0.0
+    )
+    cross_place[...] = cross.astype(bf16)
+    count = jnp.sum(jnp.broadcast_to(crossing, (8, requests)), axis=1, keepdims=True)
+    over = jnp.where(jnp.broadcast_to(count, (8, 128)) > limit + 0.5, 1.0, 0.0)
+    over_out[...] = over
+    over_in[me] = over
+    label_cross_out[...] = lax.dot_general(
+        cross_place[...], far_flags, nt, preferred_element_type=f32
+    ).astype(bf16)
+    direct_labels = lax.dot_general(
+        direct_place[...], near_flags, nt, preferred_element_type=f32
+    )
+    label_direct_out[...] = direct_labels.astype(bf16).reshape(inner, per_owner, 128)
+    label_received[plane, lane] = label_direct_out[mine]
+
+    pl.semaphore_wait(barrier, n - 1 + reps - 1)
+
+    b_mine = lax.rem(plane, 2)
+    cross_copy(None, b_mine).start()
+
+    @pl.loop(0, chunks)
+    def _(c):
+        hidden_load(c).wait()
+        cross_out[c] = jnp.dot(
+            cross_place[...], hidden[c], preferred_element_type=f32
+        ).astype(bf16)
+        cross_copy(c, b_mine).start()
+        rows = jnp.dot(direct_place[...], hidden[c], preferred_element_type=f32)
+        direct_out[c] = rows.astype(bf16).reshape(inner, per_owner, width)
+        self_copy(c).start()
+
+        @pl.loop(1, inner)
+        def _(k):
+            direct_copy(c, k).start()
+
+    @pl.loop(1, inner)
+    def _(k):
+        direct_copy(None, k).start()
+
+    @pl.loop(1, n)
+    def _(k):
+        over_copy(k).start()
+
+    direct_t[...] = direct.T.astype(bf16)
+    cross_t[...] = cross.T.astype(bf16)
+    up[...] = jnp.zeros_like(up)
+    for g in range(kept):
+        for t in range(2):
+            up[pl.ds((2 * g + t) * rank, rank), pl.ds(t * head, head)] = up_ref[g, t]
+    project[...] = jnp.zeros_like(project)
+    for h in range(heads):
+        queries[:, h, :] = queries_ref[:, pl.ds(h * head, head)].astype(f32)
+    cache_load.wait()
+    context = cache.shape[1]
+    group = 8 if requests % 8 == 0 else 1
+
+    @pl.loop(0, requests // group)
+    def _(i):
+        for u in range(group):
+            r = i * group + u
+            scores = lax.dot_general(
+                queries[r].astype(bf16),
+                cache[r, :, pl.ds(0, head)],
+                nt,
+                preferred_element_type=f32,
+            ) / math.sqrt(head)
+            usable = lax.broadcasted_iota(jnp.int32, (heads, context), 1) < lengths_ref[r]
+            scores = jnp.where(usable, scores, -1e30)
+            top = jnp.max(scores, axis=1, keepdims=True)
+            powers = jnp.where(usable, jnp.exp(scores - top), 0.0)
+            highest[r] = jnp.broadcast_to(top, (heads, head))
+            total[r] = jnp.broadcast_to(jnp.sum(powers, axis=1, keepdims=True), (heads, head))
+            context_sum[r] = jnp.dot(
+                powers.astype(bf16), cache[r, :, pl.ds(head, head)], preferred_element_type=f32
+            )
+
+    for g in range(kept):
+        down_load(g).wait()
+
+    @pl.when(is_relay)
+    def _():
+        for b in range(2):
+            cross_copy(None, b).wait_recv()
+            arrived = label_cross_in[b]
+            sorted_rows = spread(
+                lax.dot_general(grouping, arrived, nt, preferred_element_type=f32)
+            )
+            relay_place[b] = sorted_rows.astype(bf16)
+            relay_t[b] = sorted_rows.T.astype(bf16)
+            handed = jnp.dot(relay_place[b], arrived, preferred_element_type=f32)
+            label_forward[:, b] = handed.astype(bf16).reshape(inner, per_owner, 128)
+
+        @pl.loop(1, inner)
+        def _(k):
+            forward_copy(None, k, lane).start()
+
+        label_received[pl.ds(far, 2), lane] = label_forward[mine]
+
+    def relay(c):
+        @pl.when(is_relay)
+        def _():
+            for b in range(2):
+                cross_copy(c, b).wait_recv()
+                handed = jnp.dot(relay_place[b], cross_in[c, b], preferred_element_type=f32)
+                forward[c, :, b] = handed.astype(bf16).reshape(inner, per_owner, width)
+
+            @pl.loop(1, inner)
+            def _(k):
+                forward_copy(c, k, lane).start()
+
+            self_forward(c).start()
+
+    def await_forwards(c):
+        for from_lane in range(lanes):
+
+            @pl.when(relay_row + from_lane != me)
+            def _():
+                forward_copy(c, 1, from_lane).wait_recv()
+
+    def consume(c):
+        self_copy(c).wait()
+
+        @pl.loop(1, inner)
+        def _(k):
+            direct_copy(c, k).wait_recv()
+
+        await_forwards(c)
+
+        @pl.when(is_relay)
+        def _():
+            self_forward(c).wait()
+
+        project[...] += jnp.dot(
+            received[c].reshape(slots, width), down[columns(c), :], preferred_element_type=f32
+        )
+
+    relay(0)
+    relay(1)
+
+    @pl.loop(2, chunks)
+    def _(c):
+        relay(c)
+        consume(c - 2)
+
+    @pl.loop(1, n)
+    def _(k):
+        over_copy(k).wait_recv()
+
+    over_rep_out[...] = jnp.max(over_in[...], axis=0)
+    over_rep_in[rep] = over_rep_out[...]
+    for k in range(1, reps):
+        rep_copy(k).start()
+
+    consume(chunks - 2)
+
+    @pl.loop(1, inner)
+    def _(k):
+        direct_copy(None, k).wait_recv()
+
+    await_forwards(None)
+    own = lax.broadcasted_iota(jnp.int32, (128, 128), 0) - mine * kept
+    select = jnp.where(own == lax.broadcasted_iota(jnp.int32, (128, 128), 1), 1.0, 0.0)
+    picked = jnp.dot(
+        label_received[...].reshape(slots, 128), select.astype(bf16), preferred_element_type=f32
+    )
+    for k in range(1, reps):
+        rep_copy(k).wait_recv()
+    over_ref[...] = jnp.max(over_rep_in[...], axis=0)
+    consume(chunks - 1)
+
+    masked = [
+        project[:, pl.ds(g * 2 * rank, 2 * rank)] * picked[:, g : g + 1] for g in range(kept)
+    ]
+    computed = jnp.dot(
+        jnp.concatenate(masked, axis=1).astype(bf16), up[...], preferred_element_type=f32
+    )
+    update[...] = computed.astype(bf16).reshape(4, lanes, per_owner, 2 * head)
+
+    for to_lane in range(lanes):
+
+        @pl.when(relay_row + to_lane != me)
+        def _():
+            relay_copy(to_lane, mine).start()
+
+    @pl.loop(1, inner)
+    def _(k):
+        update_copy(k).start()
+
+    update_direct[mine] = update[plane, lane]
+
+    @pl.when(is_relay)
+    def _():
+        update_relay[mine] = update[pl.ds(far, 2), lane]
+
+        @pl.loop(1, inner)
+        def _(k):
+            relay_copy(lane, lax.rem(mine + k, inner)).wait_recv()
+
+        for b in range(2):
+            back_out[b] = jnp.dot(
+                relay_t[b],
+                update_relay[:, b].reshape(half_slots, 2 * head),
+                preferred_element_type=f32,
+            ).astype(bf16)
+            back_copy(b).start()
+
+    @pl.loop(1, inner)
+    def _(k):
+        update_copy(k).wait_recv()
+
+    returned = jnp.dot(
+        direct_t[...],
+        update_direct[...].reshape(half_slots, 2 * head),
+        preferred_element_type=f32,
+    )
+    back_copy(0).wait_recv()
+    returned = returned + jnp.dot(cross_t[...], back_in[...], preferred_element_type=f32)
+    entry = (fresh_ref[...].astype(f32) + returned).astype(bf16)
+    entry_ref[...] = entry
+    key = entry[:, :head].astype(f32)
+    value = entry[:, head:].astype(f32)
+    fresh_score = jnp.sum(queries[...] * key[:, None, :], axis=2, keepdims=True) / math.sqrt(head)
+    old = highest[...]
+    new = jnp.maximum(old, fresh_score)
+    scale = jnp.exp(old - new)
+    fresh_power = jnp.exp(fresh_score - new)
+    context_sum[...] = (context_sum[...] * scale + fresh_power * value[:, None, :]) / (
+        total[...] * scale + fresh_power
+    )
+    for h in range(heads):
+        attended_ref[:, pl.ds(h * head, head)] = context_sum[:, h, :].astype(bf16)
+
+    cross_copy(None, b_mine).wait_send()
+
+    @pl.loop(0, chunks)
+    def _(c):
+        cross_copy(c, b_mine).wait_send()
+
+    @pl.loop(1, inner)
+    def _(k):
+        direct_copy(None, k).wait_send()
+        update_copy(k).wait_send()
+
+        @pl.loop(0, chunks)
+        def _(c):
+            direct_copy(c, k).wait_send()
+
+    @pl.when(is_relay)
+    def _():
+        @pl.loop(1, inner)
+        def _(k):
+            forward_copy(None, k, lane).wait_send()
+
+            @pl.loop(0, chunks)
+            def _(c):
+                forward_copy(c, k, lane).wait_send()
+
+        for b in range(2):
+            back_copy(b).wait_send()
+
+    for to_lane in range(lanes):
+
+        @pl.when(relay_row + to_lane != me)
+        def _():
+            relay_copy(to_lane, mine).wait_send()
+
+    @pl.loop(1, n)
+    def _(k):
+        over_copy(k).wait_send()
+
+    for k in range(1, reps):
+        rep_copy(k).wait_send()
+
+
+def by_halves(
+    normed_hidden,
+    fresh_queries,
+    fresh_key_value,
+    key_value_cache,
+    lengths,
+    adapter_choice,
+    low_rank_down,
+    low_rank_up,
+):
+    n = lax.axis_size("wide")
+    reps = lax.axis_size("rep")
+    requests, model = normed_hidden.shape
+    per_owner = 2 * requests // n
+    kept, _, double_rank = low_rank_down.shape
+    head = low_rank_up.shape[3]
+    heads = fresh_queries.shape[1] // head
+    context = key_value_cache.shape[1]
+    slots = n * per_owner
+    inner, lanes = n // 2, n // 4
+    chunks, limit = HALF_CHUNKS, 3 * requests // 4
+    width = model // chunks
+    bf16, f32 = jnp.bfloat16, jnp.float32
+    vmem = pl.BlockSpec(memory_space=pltpu.VMEM)
+    smem = pl.BlockSpec(memory_space=pltpu.SMEM)
+    anywhere = pl.BlockSpec(memory_space=pl.ANY)
+    dma = pltpu.SemaphoreType.DMA
+    return pl.pallas_call(
+        functools.partial(half_kernel, n, reps),
+        out_shape=(
+            jax.ShapeDtypeStruct((requests, 2 * head), bf16),
+            jax.ShapeDtypeStruct((requests, heads * head), bf16),
+            jax.ShapeDtypeStruct((8, 128), f32),
+        ),
+        in_specs=[vmem, smem, anywhere, vmem, vmem, anywhere, anywhere, vmem],
+        out_specs=(vmem, vmem, vmem),
+        scratch_shapes=[
+            pltpu.VMEM((chunks, requests, width), bf16),
+            pltpu.VMEM((requests, context, 2 * head), bf16),
+            pltpu.VMEM((model, kept * double_rank), bf16),
+            pltpu.VMEM((kept * double_rank, 2 * head), bf16),
+            pltpu.VMEM((chunks, limit, width), bf16),
+            pltpu.VMEM((chunks, 2, limit, width), bf16),
+            pltpu.VMEM((chunks, inner, per_owner, width), bf16),
+            pltpu.VMEM((chunks, inner, 2, per_owner, width), bf16),
+            pltpu.VMEM((chunks, 4, lanes, per_owner, width), bf16),
+            pltpu.VMEM((limit, 128), bf16),
+            pltpu.VMEM((2, limit, 128), bf16),
+            pltpu.VMEM((inner, per_owner, 128), bf16),
+            pltpu.VMEM((inner, 2, per_owner, 128), bf16),
+            pltpu.VMEM((4, lanes, per_owner, 128), bf16),
+            pltpu.VMEM((4, lanes, per_owner, 2 * head), bf16),
+            pltpu.VMEM((inner, per_owner, 2 * head), bf16),
+            pltpu.VMEM((inner, 2, per_owner, 2 * head), bf16),
+            pltpu.VMEM((2, limit, 2 * head), bf16),
+            pltpu.VMEM((limit, 2 * head), bf16),
+            pltpu.VMEM((8, 128), f32),
+            pltpu.VMEM((n, 8, 128), f32),
+            pltpu.VMEM((8, 128), f32),
+            pltpu.VMEM((reps, 8, 128), f32),
+            pltpu.VMEM((inner * per_owner, requests), bf16),
+            pltpu.VMEM((requests, inner * per_owner), bf16),
+            pltpu.VMEM((limit, requests), bf16),
+            pltpu.VMEM((requests, limit), bf16),
+            pltpu.VMEM((2, inner * per_owner, limit), bf16),
+            pltpu.VMEM((2, limit, inner * per_owner), bf16),
+            pltpu.VMEM((requests, heads, head), f32),
+            pltpu.VMEM((requests, heads, head), f32),
+            pltpu.VMEM((requests, heads, head), f32),
+            pltpu.VMEM((requests, heads, head), f32),
+            pltpu.VMEM((slots, kept * double_rank), f32),
+            dma((chunks + kept + 1,)),
+            dma((2, chunks)),
+            dma((chunks + 1,)),
+            dma((chunks + 1, 2)),
+            dma((chunks + 1, inner)),
+            dma((chunks + 1, inner)),
+            dma((chunks + 1, inner)),
+            dma((chunks + 1, lanes)),
+            dma((inner,)),
+            dma((inner,)),
+            dma((lanes,)),
+            dma((inner,)),
+            dma((2,)),
+            dma((1,)),
+            dma((n,)),
+            dma((n,)),
+            dma((reps,)),
+            dma((reps,)),
+        ],
+        compiler_params=pltpu.CompilerParams(
+            collective_id=1, has_side_effects=True, vmem_limit_bytes=60 * 1024 * 1024
+        ),
+    )(
+        adapter_choice.reshape(1, requests),
+        lengths,
+        normed_hidden,
+        fresh_queries,
+        fresh_key_value,
+        key_value_cache,
+        low_rank_down,
+        low_rank_up,
+    )
+
+
 def device_step(*blocks):
     requests = blocks[0].shape[0]
-    per_owner = 2 * requests // lax.axis_size("wide")
-    if per_owner % 16:
+    n = lax.axis_size("wide")
+    per_owner = 2 * requests // n
+    if per_owner % 16 or n != 16:
         return shards(*blocks)
-    return fused(*blocks)
+    entry, attended, over = by_halves(*blocks)
+    return lax.cond(over[0, 0] > 0.5, lambda: fused(*blocks), lambda: (entry, attended))
 
 
 def solution(mesh):

time: 114 us -> 109 us (0.956)
  Pallas kernels: 110 us -> 104 us
    pallas_call x1, Pallas kernels: 110 us -> 104 us  [by_halves(): pl.pallas_call(functools.partial(half_kernel, n, reps), out_shape=(jax.Sh...]
    unnamed x2 -> x14, local copies, waits for them, and re-layouts: 3.14 us -> 1.36 us
    slice x0 -> x1, local copies, waits for them, and re-layouts: none -> 1.18 us  [device_step(): over[0, 0] > 0.5]
where the time goes in v2:
time: 109 us; the launch traced here: 108 us
  Pallas kernels  104 us (95%)
  local copies, waits for them, and re-layouts  2.54 us (2%)
  between operations  1.4 us (1%)
    pallas_call x1, Pallas kernels, by_halves(): pl.pallas_call(functools.partial(half_kernel, n, reps), out_shape=(jax.Sh...  104 us

profile of v2, /device:TPU:0, one launch (start us, length us, event | category | flops | bytes accessed | tf_op | source)
XLA Modules:
  0.0 108.4 jit_solution(15234596715408492230)
XLA Ops:
  0.6 0.0 copy-start
  0.6 0.0 copy-start.1
  0.7 0.0 copy-start.2
  0.7 0.0 copy-start.3
  0.7 0.0 copy-start.4
  0.7 0.0 copy-start.5
  0.7 104.4 %shard_map.99 = (bf16[128,256]{1,0:T(8,128)(2,1)S(1)}, bf16[128,1024]{1,0:T(8,128)(2,1)S(1)}, f32[8,128]{1,0:T(8,128)}) custom-call(s32[1,128]{1,0:T(1,128)} %bitcast.3, s32[128]{0:T(128)} %lengths_ref.1, bf16[128,8192]{1,0:T(8,128)(2,1)} %hidden_ref.1, bf16[128,1024]{1,0:T(8,128)(2,1)} %queries_ref.1, bf16[128,256]{1,0:T(8,128)(2,1)} %fresh_ref.1, ...), custom_call_target="tpu_custom_call" | custom-call | tf_op jit(solution)/shard_map/pallas_call | solution.py:995
  105.1 1.2 %slice.3 = f32[1,1]{1,0:T(1,128)} slice(f32[8,128]{1,0:T(8,128)} %get-tuple-element.33), slice={[0:1], [0:1]} | slice | bytes 8 | tf_op jit(solution)/shard_map/slice | solution.py:1080
  107.0 0.0 copy-done
  107.0 0.0 copy-done.1
  107.0 0.0 copy-done.2
  107.0 0.0 copy-done.3
  107.0 0.0 copy-done.4
  107.0 0.0 copy-done.5
  107.0 0.6 copy.20
  107.7 0.7 copy.21
  (1 shorter events, 0.0 us)
Async XLA Ops:
  0.6 106.3 %copy-start = (bf16[128,8192]{1,0:T(8,128)(2,1)S(1)}, bf16[128,8192]{1,0:T(8,128)(2,1)}, u32[]{:S(2)}) copy-start(bf16[128,8192]{1,0:T(8,128)(2,1)} %hidden_ref.1) | copy-start | bytes 6291460
  0.6 106.3 %copy-start.1 = (bf16[128,1024]{1,0:T(8,128)(2,1)S(1)}, bf16[128,1024]{1,0:T(8,128)(2,1)}, u32[]{:S(2)}) copy-start(bf16[128,1024]{1,0:T(8,128)(2,1)} %queries_ref.1) | copy-start | bytes 786436
  0.7 106.3 %copy-start.2 = (bf16[4,2,64,128]{3,2,1,0:T(8,128)(2,1)S(1)}, bf16[4,2,64,128]{3,2,1,0:T(8,128)(2,1)}, u32[]{:S(2)}) copy-start(bf16[4,2,64,128]{3,2,1,0:T(8,128)(2,1)} %up_ref.1) | copy-start | bytes 393220
  0.7 106.3 %copy-start.3 = (bf16[128,256]{1,0:T(8,128)(2,1)S(1)}, bf16[128,256]{1,0:T(8,128)(2,1)}, u32[]{:S(2)}) copy-start(bf16[128,256]{1,0:T(8,128)(2,1)} %fresh_ref.1) | copy-start | bytes 196612
  0.7 106.3 %copy-start.4 = (s32[128]{0:T(128)S(1)}, s32[128]{0:T(128)}, u32[]{:S(2)}) copy-start(s32[128]{0:T(128)} %param.15) | copy-start | bytes 1540
  0.7 106.3 %copy-start.5 = (s32[128]{0:T(128)S(1)}, s32[128]{0:T(128)}, u32[]{:S(2)}) copy-start(s32[128]{0:T(128)} %lengths_ref.1) | copy-start | bytes 1540

commit v3 on v2

--- a/solution.py
+++ b/solution.py
@@ -460,26 +460,17 @@
     direct_out,
     forward,
     received,
-    label_cross_out,
-    label_cross_in,
-    label_direct_out,
-    label_forward,
-    label_received,
-    update,
-    update_direct,
-    update_relay,
-    back_out,
-    back_in,
-    over_out,
-    over_in,
+    labels_out,
+    labels_in,
+    update_out,
+    update_in,
     over_rep_out,
     over_rep_in,
-    direct_place,
-    direct_t,
+    placing,
+    placing_t,
     cross_place,
-    cross_t,
+    relay_out,
     relay_place,
-    relay_t,
     queries,
     context_sum,
     highest,
@@ -493,14 +484,10 @@
     direct_recv,
     forward_send,
     forward_recv,
+    label_send,
+    label_recv,
     update_send,
     update_recv,
-    relay_send,
-    relay_recv,
-    back_send,
-    back_recv,
-    over_send,
-    over_recv,
     rep_send,
     rep_recv,
 ):
@@ -513,7 +500,6 @@
     heads = queries.shape[1]
     slots = n * per_owner
     half_slots = inner * per_owner
-    half_adapters = inner * kept
     f32, bf16 = jnp.float32, jnp.bfloat16
     nt = (((1,), (1,)), ((), ()))
 
@@ -526,6 +512,7 @@
     far = (1 - half) * 2
     is_relay = plane == 1 + half
     relay_row = (1 + half) * lanes
+    b_mine = lax.rem(plane, 2)
 
     def columns(c):
         return pl.ds(pl.multiple_of(c * width, width), width)
@@ -580,33 +567,53 @@
     def peer(k):
         return half * inner + lax.rem(mine + k, inner)
 
+    def matrix_copy(b):
+        return remote(
+            relay_out,
+            relay_place.at[b],
+            cross_send.at[chunks],
+            cross_recv.at[chunks, b],
+            (2 - half) * lanes + lane,
+        )
+
     def cross_copy(c, b):
-        source = label_cross_out if c is None else cross_out.at[c]
-        target = label_cross_in.at[b] if c is None else cross_in.at[c, b]
-        t = chunks if c is None else c
         return remote(
-            source, target, cross_send.at[t], cross_recv.at[t, b], (2 - half) * lanes + lane
+            cross_out.at[c],
+            cross_in.at[c, b],
+            cross_send.at[c],
+            cross_recv.at[c, b],
+            (2 - half) * lanes + lane,
         )
 
     def direct_copy(c, k):
         to = peer(k)
-        there = lax.rem(to, inner)
-        source = label_direct_out.at[there] if c is None else direct_out.at[c, there]
-        target = label_received.at[plane, lane] if c is None else received.at[c, plane, lane]
-        t = chunks if c is None else c
-        return remote(source, target, direct_send.at[t, k], direct_recv.at[t, k], to)
+        return remote(
+            direct_out.at[c, lax.rem(to, inner)],
+            received.at[c, plane, lane],
+            direct_send.at[c, k],
+            direct_recv.at[c, k],
+            to,
+        )
 
     def forward_copy(c, k, from_lane):
         to = peer(k)
-        there = lax.rem(to, inner)
-        source = label_forward.at[there] if c is None else forward.at[c, there]
-        rows = pl.ds(far, 2)
-        if c is None:
-            target = label_received.at[rows, from_lane]
-        else:
-            target = received.at[c, rows, from_lane]
-        t = chunks if c is None else c
-        return remote(source, target, forward_send.at[t, k], forward_recv.at[t, from_lane], to)
+        return remote(
+            forward.at[c, lax.rem(to, inner)],
+            received.at[c, pl.ds(far, 2), from_lane],
+            forward_send.at[c, k],
+            forward_recv.at[c, from_lane],
+            to,
+        )
+
+    def label_copy(k):
+        to = lax.rem(me + k, n)
+        return remote(labels_out.at[to], labels_in.at[me], label_send.at[k], label_recv.at[k], to)
+
+    def update_copy(k):
+        to = lax.rem(me + k, n)
+        return remote(
+            update_out.at[to], update_in.at[me], update_send.at[k], update_recv.at[k], to
+        )
 
     def self_copy(c):
         return pltpu.make_async_copy(
@@ -616,35 +623,6 @@
     def self_forward(c):
         return pltpu.make_async_copy(
             forward.at[c, mine], received.at[c, pl.ds(far, 2), lane], self_sem.at[1, c]
-        )
-
-    def update_copy(k):
-        to = peer(k)
-        return remote(
-            update.at[to // lanes, lax.rem(to, lanes)],
-            update_direct.at[mine],
-            update_send.at[k],
-            update_recv.at[k],
-            to,
-        )
-
-    def relay_copy(to_lane, owner):
-        return remote(
-            update.at[pl.ds(far, 2), to_lane],
-            update_relay.at[owner],
-            relay_send.at[to_lane],
-            relay_recv.at[owner],
-            relay_row + to_lane,
-        )
-
-    def back_copy(b):
-        return remote(
-            back_out.at[b], back_in, back_send.at[b], back_recv.at[0], (far + b) * lanes + lane
-        )
-
-    def over_copy(k):
-        return remote(
-            over_out, over_in.at[me], over_send.at[k], over_recv.at[k], lax.rem(me + k, n)
         )
 
     def rep_copy(k):
@@ -658,9 +636,8 @@
         )
 
     def ranks(hit):
-        size = hit.shape[1]
-        before = lax.broadcasted_iota(jnp.int32, (size, size), 0)
-        after = lax.broadcasted_iota(jnp.int32, (size, size), 1)
+        before = lax.broadcasted_iota(jnp.int32, (requests, requests), 0)
+        after = lax.broadcasted_iota(jnp.int32, (requests, requests), 1)
         earlier = jnp.dot(
             hit.astype(bf16),
             jnp.where(before < after, 1.0, 0.0).astype(bf16),
@@ -668,74 +645,65 @@
         )
         return jnp.where(hit > 0.5, earlier, -1.0).astype(jnp.int32)
 
-    def spread(hit):
-        size = hit.shape[1]
-        place = lax.broadcasted_iota(jnp.int32, (inner, per_owner, size), 1)
-        chosen = jnp.where(place == ranks(hit)[:, None, :], 1.0, 0.0)
-        return chosen.reshape(half_slots, size)
-
     ids = ids_ref[...]
-    near = ids - half * half_adapters
-    group_of = lax.broadcasted_iota(jnp.int32, (inner, 128), 1)
-    first = lax.broadcasted_iota(jnp.int32, (inner, 128), 0) * kept
+    adapter = lax.broadcasted_iota(jnp.int32, (n * kept, requests), 0)
+    named = jnp.where(adapter == ids, 1.0, 0.0).astype(bf16)
+    group_of = lax.broadcasted_iota(jnp.int32, (n, n * kept), 1)
+    first = lax.broadcasted_iota(jnp.int32, (n, n * kept), 0) * kept
     grouping = jnp.where((group_of >= first) & (group_of < first + kept), 1.0, 0.0).astype(bf16)
-    label_lane = lax.broadcasted_iota(jnp.int32, (128, requests), 0)
-    near_flags = jnp.where(label_lane == near, 1.0, 0.0).astype(bf16)
-    far_flags = jnp.where(
-        label_lane == ids - (1 - half) * half_adapters, 1.0, 0.0
+    hit = jnp.dot(grouping, named, preferred_element_type=f32)
+    place = lax.broadcasted_iota(jnp.int32, (n, per_owner, requests), 1)
+    chosen = jnp.where(place == ranks(hit)[:, None, :], 1.0, 0.0).reshape(slots, requests)
+    placing[...] = chosen.astype(bf16)
+    owner = lax.broadcasted_iota(jnp.int32, (n, requests), 0)
+    across = jnp.where((owner >= (1 - half) * inner) & (owner < (2 - half) * inner), hit, 0.0)
+    crossing = jnp.broadcast_to(jnp.sum(across, axis=0, keepdims=True), (8, requests))
+    cross = jnp.where(
+        lax.broadcasted_iota(jnp.int32, (limit, requests), 0) == ranks(crossing)[0:1, :], 1.0, 0.0
+    )
+    cross_place[...] = cross.astype(bf16)
+    near_rows = pl.ds(pl.multiple_of(half * half_slots, half_slots), half_slots)
+    far_rows = pl.ds(pl.multiple_of((1 - half) * half_slots, half_slots), half_slots)
+    relay_out[...] = lax.dot_general(
+        placing[far_rows, :], cross_place[...], nt, preferred_element_type=f32
     ).astype(bf16)
-    hit = jnp.dot(grouping, near_flags, preferred_element_type=f32)
-    direct = spread(hit)
-    direct_place[...] = direct.astype(bf16)
-    crossing = 1.0 - jnp.sum(hit, axis=0, keepdims=True)
-    cross_rank = ranks(jnp.broadcast_to(crossing, (8, requests)))[0:1, :]
-    cross = jnp.where(
-        lax.broadcasted_iota(jnp.int32, (limit, requests), 0) == cross_rank, 1.0, 0.0
-    )
-    cross_place[...] = cross.astype(bf16)
-    count = jnp.sum(jnp.broadcast_to(crossing, (8, requests)), axis=1, keepdims=True)
-    over = jnp.where(jnp.broadcast_to(count, (8, 128)) > limit + 0.5, 1.0, 0.0)
-    over_out[...] = over
-    over_in[me] = over
-    label_cross_out[...] = lax.dot_general(
-        cross_place[...], far_flags, nt, preferred_element_type=f32
-    ).astype(bf16)
-    direct_labels = lax.dot_general(
-        direct_place[...], near_flags, nt, preferred_element_type=f32
-    )
-    label_direct_out[...] = direct_labels.astype(bf16).reshape(inner, per_owner, 128)
-    label_received[plane, lane] = label_direct_out[mine]
 
     pl.semaphore_wait(barrier, n - 1 + reps - 1)
-
-    b_mine = lax.rem(plane, 2)
-    cross_copy(None, b_mine).start()
+    matrix_copy(b_mine).start()
 
     @pl.loop(0, chunks)
     def _(c):
         hidden_load(c).wait()
+        rows = jnp.dot(placing[near_rows, :], hidden[c], preferred_element_type=f32)
+        direct_out[c] = rows.astype(bf16).reshape(inner, per_owner, width)
+        self_copy(c).start()
+
+        @pl.loop(1, inner)
+        def _(k):
+            direct_copy(c, k).start()
+
         cross_out[c] = jnp.dot(
             cross_place[...], hidden[c], preferred_element_type=f32
         ).astype(bf16)
         cross_copy(c, b_mine).start()
-        rows = jnp.dot(direct_place[...], hidden[c], preferred_element_type=f32)
-        direct_out[c] = rows.astype(bf16).reshape(inner, per_owner, width)
-        self_copy(c).start()
-
-        @pl.loop(1, inner)
-        def _(k):
-            direct_copy(c, k).start()
-
-    @pl.loop(1, inner)
-    def _(k):
-        direct_copy(None, k).start()
-
-    @pl.loop(1, n)
-    def _(k):
-        over_copy(k).start()
-
-    direct_t[...] = direct.T.astype(bf16)
-    cross_t[...] = cross.T.astype(bf16)
+
+    owner_row = jnp.sum(hit * owner.astype(f32), axis=0, keepdims=True)
+    within = ids - kept * owner_row.astype(jnp.int32)
+    label_lane = lax.broadcasted_iota(jnp.int32, (128, requests), 0)
+    flags = jnp.where(label_lane == within, 1.0, 0.0).astype(bf16)
+    labels = lax.dot_general(placing[...], flags, nt, preferred_element_type=f32)
+    count = jnp.sum(crossing, axis=1, keepdims=True)[0:1, :]
+    over = jnp.where(count > limit + 0.5, 1.0, 0.0)
+    last = lax.broadcasted_iota(jnp.int32, (slots, 128), 1) == 127
+    labels = jnp.where(last, jnp.broadcast_to(over, (slots, 128)), labels)
+    labels_out[...] = labels.astype(bf16).reshape(n, per_owner, 128)
+    labels_in[me] = labels_out[me]
+
+    @pl.loop(1, n)
+    def _(k):
+        label_copy(k).start()
+
+    placing_t[...] = chosen.T.astype(bf16)
     up[...] = jnp.zeros_like(up)
     for g in range(kept):
         for t in range(2):
@@ -745,27 +713,8 @@
         queries[:, h, :] = queries_ref[:, pl.ds(h * head, head)].astype(f32)
     cache_load.wait()
     context = cache.shape[1]
-    group = 8 if requests % 8 == 0 else 1
-
-    @pl.loop(0, requests // group)
-    def _(i):
-        for u in range(group):
-            r = i * group + u
-            scores = lax.dot_general(
-                queries[r].astype(bf16),
-                cache[r, :, pl.ds(0, head)],
-                nt,
-                preferred_element_type=f32,
-            ) / math.sqrt(head)
-            usable = lax.broadcasted_iota(jnp.int32, (heads, context), 1) < lengths_ref[r]
-            scores = jnp.where(usable, scores, -1e30)
-            top = jnp.max(scores, axis=1, keepdims=True)
-            powers = jnp.where(usable, jnp.exp(scores - top), 0.0)
-            highest[r] = jnp.broadcast_to(top, (heads, head))
-            total[r] = jnp.broadcast_to(jnp.sum(powers, axis=1, keepdims=True), (heads, head))
-            context_sum[r] = jnp.dot(
-                powers.astype(bf16), cache[r, :, pl.ds(head, head)], preferred_element_type=f32
-            )
+    group = 8
+    batches = requests // group // chunks
 
     for g in range(kept):
         down_load(g).wait()
@@ -773,21 +722,7 @@
     @pl.when(is_relay)
     def _():
         for b in range(2):
-            cross_copy(None, b).wait_recv()
-            arrived = label_cross_in[b]
-            sorted_rows = spread(
-                lax.dot_general(grouping, arrived, nt, preferred_element_type=f32)
-            )
-            relay_place[b] = sorted_rows.astype(bf16)
-            relay_t[b] = sorted_rows.T.astype(bf16)
-            handed = jnp.dot(relay_place[b], arrived, preferred_element_type=f32)
-            label_forward[:, b] = handed.astype(bf16).reshape(inner, per_owner, 128)
-
-        @pl.loop(1, inner)
-        def _(k):
-            forward_copy(None, k, lane).start()
-
-        label_received[pl.ds(far, 2), lane] = label_forward[mine]
+            matrix_copy(b).wait_recv()
 
     def relay(c):
         @pl.when(is_relay)
@@ -827,38 +762,52 @@
             received[c].reshape(slots, width), down[columns(c), :], preferred_element_type=f32
         )
 
+    def attend_slice(c):
+        @pl.loop(c * batches, (c + 1) * batches)
+        def _(i):
+            for u in range(group):
+                r = i * group + u
+                scores = lax.dot_general(
+                    queries[r].astype(bf16),
+                    cache[r, :, pl.ds(0, head)],
+                    nt,
+                    preferred_element_type=f32,
+                ) / math.sqrt(head)
+                usable = lax.broadcasted_iota(jnp.int32, (heads, context), 1) < lengths_ref[r]
+                scores = jnp.where(usable, scores, -1e30)
+                top = jnp.max(scores, axis=1, keepdims=True)
+                powers = jnp.where(usable, jnp.exp(scores - top), 0.0)
+                highest[r] = jnp.broadcast_to(top, (heads, head))
+                total[r] = jnp.broadcast_to(jnp.sum(powers, axis=1, keepdims=True), (heads, head))
+                context_sum[r] = jnp.dot(
+                    powers.astype(bf16), cache[r, :, pl.ds(head, head)], preferred_element_type=f32
+                )
+
     relay(0)
+    attend_slice(0)
     relay(1)
+    attend_slice(1)
 
     @pl.loop(2, chunks)
     def _(c):
         relay(c)
+        attend_slice(c)
         consume(c - 2)
 
     @pl.loop(1, n)
     def _(k):
-        over_copy(k).wait_recv()
-
-    over_rep_out[...] = jnp.max(over_in[...], axis=0)
+        label_copy(k).wait_recv()
+
+    picked = labels_in[...].reshape(slots, 128).astype(f32)
+    over_rep_out[...] = jnp.broadcast_to(jnp.max(picked, axis=0, keepdims=True), (8, 128))
     over_rep_in[rep] = over_rep_out[...]
     for k in range(1, reps):
         rep_copy(k).start()
 
     consume(chunks - 2)
-
-    @pl.loop(1, inner)
-    def _(k):
-        direct_copy(None, k).wait_recv()
-
-    await_forwards(None)
-    own = lax.broadcasted_iota(jnp.int32, (128, 128), 0) - mine * kept
-    select = jnp.where(own == lax.broadcasted_iota(jnp.int32, (128, 128), 1), 1.0, 0.0)
-    picked = jnp.dot(
-        label_received[...].reshape(slots, 128), select.astype(bf16), preferred_element_type=f32
-    )
     for k in range(1, reps):
         rep_copy(k).wait_recv()
-    over_ref[...] = jnp.max(over_rep_in[...], axis=0)
+    over_ref[0, 0] = jnp.max(over_rep_in[:, :, 127:128])
     consume(chunks - 1)
 
     masked = [
@@ -867,47 +816,21 @@
     computed = jnp.dot(
         jnp.concatenate(masked, axis=1).astype(bf16), up[...], preferred_element_type=f32
     )
-    update[...] = computed.astype(bf16).reshape(4, lanes, per_owner, 2 * head)
-
-    for to_lane in range(lanes):
-
-        @pl.when(relay_row + to_lane != me)
-        def _():
-            relay_copy(to_lane, mine).start()
-
-    @pl.loop(1, inner)
+    update_out[...] = computed.astype(bf16).reshape(n, per_owner, 2 * head)
+
+    @pl.loop(1, n)
     def _(k):
         update_copy(k).start()
 
-    update_direct[mine] = update[plane, lane]
-
-    @pl.when(is_relay)
-    def _():
-        update_relay[mine] = update[pl.ds(far, 2), lane]
-
-        @pl.loop(1, inner)
-        def _(k):
-            relay_copy(lane, lax.rem(mine + k, inner)).wait_recv()
-
-        for b in range(2):
-            back_out[b] = jnp.dot(
-                relay_t[b],
-                update_relay[:, b].reshape(half_slots, 2 * head),
-                preferred_element_type=f32,
-            ).astype(bf16)
-            back_copy(b).start()
-
-    @pl.loop(1, inner)
+    update_in[me] = update_out[me]
+
+    @pl.loop(1, n)
     def _(k):
         update_copy(k).wait_recv()
 
     returned = jnp.dot(
-        direct_t[...],
-        update_direct[...].reshape(half_slots, 2 * head),
-        preferred_element_type=f32,
-    )
-    back_copy(0).wait_recv()
-    returned = returned + jnp.dot(cross_t[...], back_in[...], preferred_element_type=f32)
+        placing_t[...], update_in[...].reshape(slots, 2 * head), preferred_element_type=f32
+    )
     entry = (fresh_ref[...].astype(f32) + returned).astype(bf16)
     entry_ref[...] = entry
     key = entry[:, :head].astype(f32)
@@ -923,43 +846,28 @@
     for h in range(heads):
         attended_ref[:, pl.ds(h * head, head)] = context_sum[:, h, :].astype(bf16)
 
-    cross_copy(None, b_mine).wait_send()
+    matrix_copy(b_mine).wait_send()
 
     @pl.loop(0, chunks)
     def _(c):
         cross_copy(c, b_mine).wait_send()
 
-    @pl.loop(1, inner)
-    def _(k):
-        direct_copy(None, k).wait_send()
-        update_copy(k).wait_send()
-
+        @pl.loop(1, inner)
+        def _(k):
+            direct_copy(c, k).wait_send()
+
+    @pl.when(is_relay)
+    def _():
         @pl.loop(0, chunks)
         def _(c):
-            direct_copy(c, k).wait_send()
-
-    @pl.when(is_relay)
-    def _():
-        @pl.loop(1, inner)
-        def _(k):
-            forward_copy(None, k, lane).wait_send()
-
-            @pl.loop(0, chunks)
-            def _(c):
+            @pl.loop(1, inner)
+            def _(k):
                 forward_copy(c, k, lane).wait_send()
 
-        for b in range(2):
-            back_copy(b).wait_send()
-
-    for to_lane in range(lanes):
-
-        @pl.when(relay_row + to_lane != me)
-        def _():
-            relay_copy(to_lane, mine).wait_send()
-
-    @pl.loop(1, n)
-    def _(k):
-        over_copy(k).wait_send()
+    @pl.loop(1, n)
+    def _(k):
+        label_copy(k).wait_send()
+        update_copy(k).wait_send()
 
     for k in range(1, reps):
         rep_copy(k).wait_send()
@@ -997,10 +905,10 @@
         out_shape=(
             jax.ShapeDtypeStruct((requests, 2 * head), bf16),
             jax.ShapeDtypeStruct((requests, heads * head), bf16),
-            jax.ShapeDtypeStruct((8, 128), f32),
+            jax.ShapeDtypeStruct((1, 1), f32),
         ),
         in_specs=[vmem, smem, anywhere, vmem, vmem, anywhere, anywhere, vmem],
-        out_specs=(vmem, vmem, vmem),
+        out_specs=(vmem, vmem, smem),
         scratch_shapes=[
             pltpu.VMEM((chunks, requests, width), bf16),
             pltpu.VMEM((requests, context, 2 * head), bf16),
@@ -1011,26 +919,17 @@
             pltpu.VMEM((chunks, inner, per_owner, width), bf16),
             pltpu.VMEM((chunks, inner, 2, per_owner, width), bf16),
             pltpu.VMEM((chunks, 4, lanes, per_owner, width), bf16),
-            pltpu.VMEM((limit, 128), bf16),
-            pltpu.VMEM((2, limit, 128), bf16),
-            pltpu.VMEM((inner, per_owner, 128), bf16),
-            pltpu.VMEM((inner, 2, per_owner, 128), bf16),
-            pltpu.VMEM((4, lanes, per_owner, 128), bf16),
-            pltpu.VMEM((4, lanes, per_owner, 2 * head), bf16),
-            pltpu.VMEM((inner, per_owner, 2 * head), bf16),
-            pltpu.VMEM((inner, 2, per_owner, 2 * head), bf16),
-            pltpu.VMEM((2, limit, 2 * head), bf16),
-            pltpu.VMEM((limit, 2 * head), bf16),
-            pltpu.VMEM((8, 128), f32),
-            pltpu.VMEM((n, 8, 128), f32),
+            pltpu.VMEM((n, per_owner, 128), bf16),
+            pltpu.VMEM((n, per_owner, 128), bf16),
+            pltpu.VMEM((n, per_owner, 2 * head), bf16),
+            pltpu.VMEM((n, per_owner, 2 * head), bf16),
             pltpu.VMEM((8, 128), f32),
             pltpu.VMEM((reps, 8, 128), f32),
-            pltpu.VMEM((inner * per_owner, requests), bf16),
-            pltpu.VMEM((requests, inner * per_owner), bf16),
+            pltpu.VMEM((slots, requests), bf16),
+            pltpu.VMEM((requests, slots), bf16),
             pltpu.VMEM((limit, requests), bf16),
-            pltpu.VMEM((requests, limit), bf16),
+            pltpu.VMEM((inner * per_owner, limit), bf16),
             pltpu.VMEM((2, inner * per_owner, limit), bf16),
-            pltpu.VMEM((2, limit, inner * per_owner), bf16),
             pltpu.VMEM((requests, heads, head), f32),
             pltpu.VMEM((requests, heads, head), f32),
             pltpu.VMEM((requests, heads, head), f32),
@@ -1040,16 +939,12 @@
             dma((2, chunks)),
             dma((chunks + 1,)),
             dma((chunks + 1, 2)),
-            dma((chunks + 1, inner)),
-            dma((chunks + 1, inner)),
-            dma((chunks + 1, inner)),
-            dma((chunks + 1, lanes)),
-            dma((inner,)),
-            dma((inner,)),
-            dma((lanes,)),
-            dma((inner,)),
-            dma((2,)),
-            dma((1,)),
+            dma((chunks, inner)),
+            dma((chunks, inner)),
+            dma((chunks, inner)),
+            dma((chunks, lanes)),
+            dma((n,)),
+            dma((n,)),
             dma((n,)),
             dma((n,)),
             dma((reps,)),

time: 109 us -> 102 us (0.936)
  Pallas kernels: 104 us -> 99.4 us
  local copies, waits for them, and re-layouts: 2.54 us -> 1.36 us
    pallas_call x1, Pallas kernels: 104 us -> 99.4 us  [by_halves(): pl.pallas_call(functools.partial(half_kernel, n, reps), out_shape=(jax.Sh...]
    slice x1 -> x0, local copies, waits for them, and re-layouts: 1.18 us -> none  [device_step(): over[0, 0] > 0.5]
where the time goes in v3:
time: 102 us
  Pallas kernels  99.4 us (97%)
  between operations  1.37 us (1%)
  local copies, waits for them, and re-layouts  1.36 us (1%)
    pallas_call x1, Pallas kernels, by_halves(): pl.pallas_call(functools.partial(half_kernel, n, reps), out_shape=(jax.Sh...  99.4 us

profile of v3, /device:TPU:0, one launch (start us, length us, event | category | flops | bytes accessed | tf_op | source)
XLA Modules:
  0.0 102.2 jit_solution(16727492229560550679)
XLA Ops:
  0.6 0.0 copy-start
  0.6 0.0 copy-start.1
  0.7 0.0 copy-start.2
  0.7 0.0 copy-start.3
  0.7 0.0 copy-start.4
  0.7 0.0 copy-start.5
  0.7 99.4 %shard_map.99 = (bf16[128,256]{1,0:T(8,128)(2,1)S(1)}, bf16[128,1024]{1,0:T(8,128)(2,1)S(1)}, f32[1,1]{1,0:T(1,128)}) custom-call(s32[1,128]{1,0:T(1,128)} %bitcast.3, s32[128]{0:T(128)} %lengths_ref.1, bf16[128,8192]{1,0:T(8,128)(2,1)} %hidden_ref.1, bf16[128,1024]{1,0:T(8,128)(2,1)} %queries_ref.1, bf16[128,256]{1,0:T(8,128)(2,1)} %fresh_ref.1, ...), custom_call_target="tpu_custom_call" | custom-call | tf_op jit(solution)/shard_map/pallas_call | solution.py:903
  100.7 0.0 copy-done
  100.8 0.0 copy-done.1
  100.8 0.0 copy-done.2
  100.8 0.0 copy-done.3
  100.8 0.0 copy-done.4
  100.8 0.0 copy-done.5
  100.8 0.6 copy.20
  101.5 0.7 copy.21
  (1 shorter events, 0.0 us)
Async XLA Ops:
  0.6 100.1 %copy-start = (bf16[128,8192]{1,0:T(8,128)(2,1)S(1)}, bf16[128,8192]{1,0:T(8,128)(2,1)}, u32[]{:S(2)}) copy-start(bf16[128,8192]{1,0:T(8,128)(2,1)} %hidden_ref.1) | copy-start | bytes 6291460
  0.6 100.1 %copy-start.1 = (bf16[128,1024]{1,0:T(8,128)(2,1)S(1)}, bf16[128,1024]{1,0:T(8,128)(2,1)}, u32[]{:S(2)}) copy-start(bf16[128,1024]{1,0:T(8,128)(2,1)} %queries_ref.1) | copy-start | bytes 786436
  0.7 100.1 %copy-start.2 = (bf16[4,2,64,128]{3,2,1,0:T(8,128)(2,1)S(1)}, bf16[4,2,64,128]{3,2,1,0:T(8,128)(2,1)}, u32[]{:S(2)}) copy-start(bf16[4,2,64,128]{3,2,1,0:T(8,128)(2,1)} %up_ref.1) | copy-start | bytes 393220
  0.7 100.1 %copy-start.3 = (bf16[128,256]{1,0:T(8,128)(2,1)S(1)}, bf16[128,256]{1,0:T(8,128)(2,1)}, u32[]{:S(2)}) copy-start(bf16[128,256]{1,0:T(8,128)(2,1)} %fresh_ref.1) | copy-start | bytes 196612
  0.7 100.1 %copy-start.4 = (s32[128]{0:T(128)S(1)}, s32[128]{0:T(128)}, u32[]{:S(2)}) copy-start(s32[128]{0:T(128)} %param.15) | copy-start | bytes 1540
  0.7 100.1 %copy-start.5 = (s32[128]{0:T(128)S(1)}, s32[128]{0:T(128)}, u32[]{:S(2)}) copy-start(s32[128]{0:T(128)} %lengths_ref.1) | copy-start | bytes 1540
